TPU v7x, 128 devices: a whole 4x4x4 slice. The times are simulated.
128 devices in a mesh: img: 32 (over z_lo, y, x), layer: 4 (over z_hi, core).
Axes of the slice: x: 4, y: 4, z: 4 (z_hi: 2, z_lo: 2; z = z_hi * 2 + z_lo), core: 2. Of those that a mesh axis runs over, the one named last changes fastest.
Arguments:
- checkpoint: bfloat16 [4, 16384, 2048], P('layer', 'img'), may hold values from -6 to 6
- cotangent: bfloat16 [4, 16384, 2048], P('layer', 'img')
- weights: bfloat16 [8, 2048, 2048], P('layer'), may hold values from -0.1875 to 0.1875
- partner: int32 [32], P('img'), may hold values from 0 to 31, as said below
Outputs:
- self_tile: float32 [16384, 512], P(('img', 'layer'))
- cross_tile: float32 [16384, 512], P(('img', 'layer'))
Inputs may be any that keep to these rules, and one draw needn't show every extreme that they name: partner[p] = p XOR r for one round number r with 1 <= r < 32, the same r for every p.
All inputs are finite; a program needn't handle non-finite values.
Results may differ from a plain program's by a relative error of at most 0.00051.
Values may be sent and summed in bfloat16 or wider, within the bound.
A program may use at most 128 MiB of HBM per device.

v0:
```python
import jax
import jax.numpy as jnp
from jax import lax
from jax.sharding import PartitionSpec as P


def swapped(array, axis, distance):
    return lax.ppermute(array, axis, [(i, i ^ 1 << distance) for i in range(lax.axis_size(axis))])


def derivative(z):
    s = jax.nn.sigmoid(z)
    return s * (1.0 + z * (1.0 - s))


def group_pass(start, cotan, layer_weights):
    depth = layer_weights.shape[0]
    acts = [start]
    zlist = []
    a = start
    for k in range(depth):
        z = jnp.dot(a, layer_weights[k], preferred_element_type=jnp.float32)
        zlist.append(z)
        if k < depth - 1:
            a = (z * jax.nn.sigmoid(z)).astype(jnp.bfloat16)
            acts.append(a)
    grads = [None] * depth
    upper = cotan.astype(jnp.float32)
    for k in range(depth - 1, -1, -1):
        g = (upper * derivative(zlist[k])).astype(jnp.bfloat16)
        grads[k] = g
        if k > 0:
            upper = lax.dot_general(
                g, layer_weights[k], (((1,), (1,)), ((), ())), preferred_element_type=jnp.float32
            )
    return (jnp.stack(acts), jnp.stack(grads))


def kernel_tile(acts, grads, other_acts, other_grads):
    width = acts.shape[2]
    gram_a = (
        jnp.einsum("kbd,kcd->kbc", acts, other_acts, preferred_element_type=jnp.float32) / width
    )
    gram_g = (
        jnp.einsum("kbd,kcd->kbc", grads, other_grads, preferred_element_type=jnp.float32) / width
    )
    return jnp.sum(gram_a * gram_g, axis=0)


def swap_layers(payload, bit):
    return swapped(payload, "img", bit)


def walk_bits(payload, bit_list, round_number, swapper):
    for bit in bit_list:
        taken = jnp.bitwise_and(jnp.right_shift(round_number, bit), 1) == 1
        moved = swapper(payload, bit)
        payload = jnp.where(taken, moved, payload)
    return payload


def on_device(checkpoint, cotangent, weights, partner):
    start = checkpoint[0]
    cotan = cotangent[0]
    acts, grads = group_pass(start, cotan, weights)
    self_term = kernel_tile(acts, grads, acts, grads)
    round_number = jnp.bitwise_xor(partner[0], lax.axis_index("img"))
    nbits = lax.axis_size("img").bit_length() - 1
    bit_list = list(range(nbits))
    stacked = jnp.concatenate([acts, grads], axis=0)
    stacked = walk_bits(stacked, bit_list, round_number, swap_layers)
    depth = acts.shape[0]
    other_acts = stacked[:depth]
    other_grads = stacked[depth:]
    cross_term = kernel_tile(acts, grads, other_acts, other_grads)
    self_full, cross_full = lax.psum((self_term, cross_term), "layer")
    rows = self_term.shape[0] // lax.axis_size("layer")
    offset = lax.axis_index("layer") * rows
    self_tile = lax.dynamic_slice_in_dim(self_full, offset, rows, 0)
    cross_tile = lax.dynamic_slice_in_dim(cross_full, offset, rows, 0)
    return (self_tile, cross_tile)


def solution(mesh):
    return jax.shard_map(
        on_device,
        mesh=mesh,
        in_specs=(
            P("layer", "img", None),
            P("layer", "img", None),
            P("layer", None, None),
            P("img"),
        ),
        out_specs=(P(("img", "layer"), None), P(("img", "layer"), None)),
        check_vma=False,
    )
```

profile of v0, /device:TPU:1, one launch (start us, length us, event | category | flops | bytes accessed | tf_op | source)
XLA Modules:
  0.0 1055.7 jit_solution(2415405627950097596)
XLA Ops:
  7.2 7.6 fusion.4
  16.4 8.9 fusion.13
  25.3 9.5 fusion.16
  34.9 4.0 pad_maximum_fusion
  38.9 2.0 collective-permute-start
  41.6 179.3 %collective-permute-done = bf16[4,512,2048]{2,1,0:T(8,128)(2,1)} collective-permute-done((bf16[4,512,2048]{2,1,0:T(8,128)(2,1)}, bf16[4,512,2048]{2,1,0:T(8,128)(2,1)}, u32[]{:S(2)}, u32[]{:S(2)}) %collective-permute-start) | collective-permute-done | bytes 8388640 | tf_op jit(solution)/shard_map/ppermute | solution.py:8
  220.9 6.8 broadcast_select_fusion
  227.7 3.2 collective-permute-start.1
  230.9 179.3 %collective-permute-done.1 = bf16[4,512,2048]{2,1,0:T(8,128)(2,1)} collective-permute-done((bf16[4,512,2048]{2,1,0:T(8,128)(2,1)}, bf16[4,512,2048]{2,1,0:T(8,128)(2,1)}, u32[]{:S(2)}, u32[]{:S(2)}) %collective-permute-start.1) | collective-permute-done | bytes 8388640 | tf_op jit(solution)/shard_map/ppermute | solution.py:8
  410.2 6.9 broadcast_select_fusion.1
  418.6 178.4 %collective-permute-done.2 = bf16[4,512,2048]{2,1,0:T(8,128)(2,1)} collective-permute-done((bf16[4,512,2048]{2,1,0:T(8,128)(2,1)}, bf16[4,512,2048]{2,1,0:T(8,128)(2,1)}, u32[]{:S(2)}, u32[]{:S(2)}) %collective-permute-start.2) | collective-permute-done | bytes 8388640 | tf_op jit(solution)/shard_map/ppermute | solution.py:8
  596.9 7.2 broadcast_select_fusion.2
  604.2 3.0 collective-permute-start.3
  607.2 177.5 %collective-permute-done.3 = bf16[4,512,2048]{2,1,0:T(8,128)(2,1)} collective-permute-done((bf16[4,512,2048]{2,1,0:T(8,128)(2,1)}, bf16[4,512,2048]{2,1,0:T(8,128)(2,1)}, u32[]{:S(2)}, u32[]{:S(2)}) %collective-permute-start.3) | collective-permute-done | bytes 8388640 | tf_op jit(solution)/shard_map/ppermute | solution.py:8
  784.6 7.2 broadcast_select_fusion.3
  791.9 1.7 collective-permute-start.4
  793.5 6.0 fusion.19
  799.5 3.5 multiply_reduce_fusion.1
  803.0 167.3 %collective-permute-done.4 = bf16[4,512,2048]{2,1,0:T(8,128)(2,1)} collective-permute-done((bf16[4,512,2048]{2,1,0:T(8,128)(2,1)}, bf16[4,512,2048]{2,1,0:T(8,128)(2,1)}, u32[]{:S(2)}, u32[]{:S(2)}) %collective-permute-start.4) | collective-permute-done | bytes 8388640 | tf_op jit(solution)/shard_map/ppermute | solution.py:8
  970.3 4.4 broadcast_select_fusion.4
  974.8 2.4 fusion.11
  977.2 3.7 multiply_reduce_fusion
  980.8 66.1 %all-reduce.3.cloned.1.call-done = (f32[512,512]{1,0:T(8,128)}, f32[512,512]{1,0:T(8,128)}) async-done(((f32[512,512]{1,0:T(8,128)}, f32[512,512]{1,0:T(8,128)}), (f32[512,512]{1,0:T(8,128)}, f32[512,512]{1,0:T(8,128)})) %all-reduce.3.cloned.1.call-update) | async-done | bytes 2097168 | tf_op jit(solution)/shard_map/psum | solution.py:76
  1047.0 1.9 constant_dynamic-slice_fusion
  (18 shorter events, 3.1 us)
Async XLA Ops:
  7.2 1039.8 %all-reduce.3.cloned.1.call-start = ((), (), s32[]{:S(2)}) async-start(), calls=%async_computation | async-start | bytes 4194304 | tf_op jit(solution)/shard_map/psum | solution.py:76
  14.8 1.6 copy-start.6
  25.3 9.5 copy-start.2
  25.3 9.5 copy-start
  34.8 4.0 copy-start.4
  38.9 182.0 %collective-permute-start = (bf16[4,512,2048]{2,1,0:T(8,128)(2,1)}, bf16[4,512,2048]{2,1,0:T(8,128)(2,1)}, u32[]{:S(2)}, u32[]{:S(2)}) collective-permute-start(bf16[4,512,2048]{2,1,0:T(8,128)(2,1)} %pad_maximum_fusion), channel_id=1, source_target_pairs={{0,4},{4,0},{8,12},{12,8},{16,20},{20,16},{24,28},{28,24},{32,36},... | collective-permute-start | bytes 25165832 | tf_op jit(solution)/shard_map/ppermute | solution.py:8
  227.7 182.5 %collective-permute-start.1 = (bf16[4,512,2048]{2,1,0:T(8,128)(2,1)}, bf16[4,512,2048]{2,1,0:T(8,128)(2,1)}, u32[]{:S(2)}, u32[]{:S(2)}) collective-permute-start(bf16[4,512,2048]{2,1,0:T(8,128)(2,1)} %broadcast_select_fusion), channel_id=1, source_target_pairs={{0,8},{4,12},{8,0},{12,4},{16,24},{20,28},{24,16},{28,20},{32,40},... | collective-permute-start | bytes 25165832 | tf_op jit(solution)/shard_map/ppermute | solution.py:8
  417.1 179.8 %collective-permute-start.2 = (bf16[4,512,2048]{2,1,0:T(8,128)(2,1)}, bf16[4,512,2048]{2,1,0:T(8,128)(2,1)}, u32[]{:S(2)}, u32[]{:S(2)}) collective-permute-start(bf16[4,512,2048]{2,1,0:T(8,128)(2,1)} %broadcast_select_fusion.1), channel_id=1, source_target_pairs={{0,16},{4,20},{8,24},{12,28},{16,0},{20,4},{24,8},{28,12},{32,48},... | collective-permute-start | bytes 25165832 | tf_op jit(solution)/shard_map/ppermute | solution.py:8
  604.2 180.5 %collective-permute-start.3 = (bf16[4,512,2048]{2,1,0:T(8,128)(2,1)}, bf16[4,512,2048]{2,1,0:T(8,128)(2,1)}, u32[]{:S(2)}, u32[]{:S(2)}) collective-permute-start(bf16[4,512,2048]{2,1,0:T(8,128)(2,1)} %broadcast_select_fusion.2), channel_id=1, source_target_pairs={{0,32},{4,36},{8,40},{12,44},{16,48},{20,52},{24,56},{28,60},{32,0... | collective-permute-start | bytes 25165832 | tf_op jit(solution)/shard_map/ppermute | solution.py:8
  791.9 178.5 %collective-permute-start.4 = (bf16[4,512,2048]{2,1,0:T(8,128)(2,1)}, bf16[4,512,2048]{2,1,0:T(8,128)(2,1)}, u32[]{:S(2)}, u32[]{:S(2)}) collective-permute-start(bf16[4,512,2048]{2,1,0:T(8,128)(2,1)} %broadcast_select_fusion.3), channel_id=1, source_target_pairs={{0,64},{4,68},{8,72},{12,76},{16,80},{20,84},{24,88},{28,92},{32,9... | collective-permute-start | bytes 25165832 | tf_op jit(solution)/shard_map/ppermute | solution.py:8
  793.5 6.0 copy-start.1
  974.7 2.4 copy-start.3
  974.8 2.4 copy-start.5
Sparse Core Ops, SparseCore 0:
  981.0 65.9 all-reduce.2
where the time goes:
time: 1060 us
  waiting for transfers between devices  948 us (89%)
  matrix products  41.5 us (4%)
  other arithmetic  37.7 us (4%)
  between operations  14.8 us (1%)
  starting transfers between devices  11.4 us (1%)
    ppermute x5, waiting for transfers between devices, swapped(): lax.ppermute(array, axis, [(i, i ^ 1 << distance) for i in range(lax.axis...  882 us
    psum x1, waiting for transfers between devices, on_device(): self_full, cross_full = lax.psum((self_term, cross_term), 'layer')  66.1 us
    select_n x5, other arithmetic, walk_bits(): payload = jnp.where(taken, moved, payload)  32.6 us
  transfers between devices with their start and end apart: 6, of which 6 were waited for; matrix products, arithmetic and copies ran while one was open for 1% of the time, Pallas kernels for 0%

commit v1 on v0

v1 whole, which is shorter than its diff:
```python
import functools

import jax
import jax.numpy as jnp
from jax import lax
from jax.experimental import pallas as pl
from jax.experimental.pallas import tpu as pltpu
from jax.sharding import PartitionSpec as P

MESH = pl.DeviceIdType.MESH


def paired(index, round_number):
    out = index
    bit = 0
    while round_number >> bit:
        if (round_number >> bit) & 1:
            out = out + (1 - 2 * ((index // (1 << bit)) % 2)) * (1 << bit)
        bit += 1
    return out


def swap_kernel(round_number, a_ref, c_ref, a_out, c_out, send, recv):
    other = paired(lax.axis_index("img"), round_number)
    device = (other, lax.axis_index("layer"))
    barrier = pltpu.get_barrier_semaphore()
    pl.semaphore_signal(barrier, inc=1, device_id=device, device_id_type=MESH)
    pl.semaphore_wait(barrier, 1)
    copies = [
        pltpu.make_async_remote_copy(
            src_ref=src, dst_ref=dst, send_sem=send.at[n], recv_sem=recv.at[n],
            device_id=device, device_id_type=MESH,
        )
        for n, (src, dst) in enumerate(((a_ref, a_out), (c_ref, c_out)))
    ]
    for copy in copies:
        copy.start()
    for copy in copies:
        copy.wait()


def swap(round_number, a, c):
    return pl.pallas_call(
        functools.partial(swap_kernel, round_number),
        out_shape=[jax.ShapeDtypeStruct(a.shape, a.dtype)] * 2,
        in_specs=[pl.BlockSpec(memory_space=pl.ANY)] * 2,
        out_specs=[pl.BlockSpec(memory_space=pl.ANY)] * 2,
        scratch_shapes=[pltpu.SemaphoreType.DMA((2,)), pltpu.SemaphoreType.DMA((2,))],
        compiler_params=pltpu.CompilerParams(collective_id=round_number, has_side_effects=True),
        name=f"swap_{round_number}",
    )(a, c)


def derivative(z):
    s = jax.nn.sigmoid(z)
    return s * (1.0 + z * (1.0 - s))


def group_pass(start, cotan, layer_weights):
    depth = layer_weights.shape[0]
    acts = [start]
    zlist = []
    a = start
    for k in range(depth):
        z = jnp.dot(a, layer_weights[k], preferred_element_type=jnp.float32)
        zlist.append(z)
        if k < depth - 1:
            a = (z * jax.nn.sigmoid(z)).astype(jnp.bfloat16)
            acts.append(a)
    grads = [None] * depth
    upper = cotan.astype(jnp.float32)
    for k in range(depth - 1, -1, -1):
        g = (upper * derivative(zlist[k])).astype(jnp.bfloat16)
        grads[k] = g
        if k > 0:
            upper = lax.dot_general(
                g, layer_weights[k], (((1,), (1,)), ((), ())), preferred_element_type=jnp.float32
            )
    return acts, grads


def kernel_tile(acts, grads, other_acts, other_grads):
    width = acts[0].shape[1]
    nt = (((1,), (1,)), ((), ()))
    total = 0.0
    for a, g, b, h in zip(acts, grads, other_acts, other_grads):
        gram_a = lax.dot_general(a, b, nt, preferred_element_type=jnp.float32) / width
        gram_g = lax.dot_general(g, h, nt, preferred_element_type=jnp.float32) / width
        total = total + gram_a * gram_g
    return total


def on_device(checkpoint, cotangent, weights, partner):
    start, cotan = checkpoint[0], cotangent[0]
    round_number = jnp.bitwise_xor(partner[0], lax.axis_index("img"))
    n = lax.axis_size("img")
    other_start, other_cotan = lax.switch(
        round_number - 1, [functools.partial(swap, r) for r in range(1, n)], start, cotan
    )
    acts, grads = group_pass(start, cotan, weights)
    self_term = kernel_tile(acts, grads, acts, grads)
    other_acts, other_grads = group_pass(other_start, other_cotan, weights)
    cross_term = kernel_tile(acts, grads, other_acts, other_grads)
    self_tile = lax.psum_scatter(self_term, "layer", scatter_dimension=0, tiled=True)
    cross_tile = lax.psum_scatter(cross_term, "layer", scatter_dimension=0, tiled=True)
    return (self_tile, cross_tile)


def solution(mesh):
    return jax.shard_map(
        on_device,
        mesh=mesh,
        in_specs=(
            P("layer", "img", None),
            P("layer", "img", None),
            P("layer", None, None),
            P("img"),
        ),
        out_specs=(P(("img", "layer"), None), P(("img", "layer"), None)),
        check_vma=False,
    )
```

time: 1060 us -> 220 us (0.21)
  waiting for transfers between devices: 948 us -> 35.8 us
  Pallas kernels: 0 us -> 92.3 us
  other arithmetic: 37.7 us -> 0.01 us
  matrix products: 41.5 us -> 68.1 us
  starting transfers between devices: 11.4 us -> 0.08 us
    ppermute x5 -> x0, waiting for transfers between devices: 882 us -> none  [swapped(): lax.ppermute(array, axis, [(i, i ^ 1 << distance) for i in range(lax.axis...]
    pallas_call x0 -> x1, Pallas kernels: none -> 92.3 us  [swap(): pl.pallas_call(functools.partial(swap_kernel, round_number), out_shape=[j...]
    psum x1 -> x0, waiting for transfers between devices: 66.1 us -> none  [on_device(): self_full, cross_full = lax.psum((self_term, cross_term), 'layer')]
    reduce_scatter x0 -> x2, waiting for transfers between devices: none -> 35.8 us  [the longest x1 35.7 us: on_device(): lax.psum_scatter(cross_term, 'layer', scatter_dimension=0, tiled=True)]
    select_n x5 -> x0, other arithmetic: 32.6 us -> none  [walk_bits(): payload = jnp.where(taken, moved, payload)]
    dot_general x2 -> x4, matrix products: 16.5 us -> 31.3 us  [group_pass(): z = jnp.dot(a, layer_weights[k], preferred_element_type=jnp.float32)]
    dot_general x4 -> x8, matrix products: 15.5 us -> 28.1 us  [the longest x4 17.6 us: kernel_tile(): lax.dot_general(g, h, nt, preferred_element_type=jnp.float32) / width]
    ppermute x5 -> x0, starting transfers between devices: 11.4 us -> none  [swapped(): lax.ppermute(array, axis, [(i, i ^ 1 << distance) for i in range(lax.axis...]
  transfers between devices with their start and end apart: 6 -> 2, of which waited for: 6 -> 1; matrix products, arithmetic and copies ran while one was open for 1% -> 16% of each run, Pallas kernels for 0% -> 42%
where the time goes in v1:
time: 220 us
  Pallas kernels  92.3 us (42%)
  matrix products  68.1 us (31%)
  waiting for transfers between devices  35.8 us (16%)
  between operations  14.9 us (7%)
  local copies, waits for them, and re-layouts  8.37 us (4%)
    pallas_call x1, Pallas kernels, swap(): pl.pallas_call(functools.partial(swap_kernel, round_number), out_shape=[j...  92.3 us
    reduce_scatter x1, waiting for transfers between devices, on_device(): lax.psum_scatter(cross_term, 'layer', scatter_dimension=0, tiled=True)  35.7 us
    dot_general x4, matrix products, group_pass(): z = jnp.dot(a, layer_weights[k], preferred_element_type=jnp.float32)  31.3 us
    dot_general x4, matrix products, kernel_tile(): lax.dot_general(g, h, nt, preferred_element_type=jnp.float32) / width  17.6 us
    dot_general x4, matrix products, kernel_tile(): lax.dot_general(a, b, nt, preferred_element_type=jnp.float32) / width  10.5 us
    dot_general x1, matrix products, group_pass(): lax.dot_general(g, layer_weights[k], (((1,), (1,)), ((), ())), preferred_...  8.68 us
    unnamed x40, local copies, waits for them, and re-layouts  8.37 us
  transfers between devices with their start and end apart: 2, of which 1 were waited for; matrix products, arithmetic and copies ran while one was open for 16% of the time, Pallas kernels for 42%

profile of v1, /device:TPU:1, one launch (start us, length us, event | category | flops | bytes accessed | tf_op | source)
XLA Modules:
  0.0 219.8 jit_solution(144591160060554320)
XLA Ops:
  7.2 3.7 %convolution_multiply_fusion.6 = f32[512,512]{1,0:T(8,128)S(1)} fusion(bf16[1,512,2048]{2,1,0:T(8,128)(2,1)} %param.35), kind=kOutput, calls=%fused_computation.40 | convolution fusion | flops 1074003968 | bytes 3145728 | tf_op jit(solution)/shard_map/dot_general | solution.py:87
  10.9 9.8 %multiply_convert_fusion.4 = (bf16[512,2048]{1,0:T(8,128)(2,1)S(1)}, f32[512,2048]{1,0:T(8,128)}) fusion(bf16[2,2048,2048]{2,1,0:T(8,128)(2,1)} %param.37, bf16[1,512,2048]{2,1,0:T(8,128)(2,1)S(1)} %copy-done.1), kind=kOutput, calls=%fused_computation.25 | convolution fusion | flops 4300210176 | bytes 16777216 | tf_op jit(solution)/shard_map/dot_general | solution.py:65
  20.7 1.3 convolution_multiply_fusion.4
  22.0 1.0 copy-done
  23.0 5.8 %multiply_convert_fusion.3 = bf16[512,2048]{1,0:T(8,128)(2,1)S(1)} fusion(bf16[512,2048]{1,0:T(8,128)(2,1)S(1)} %get-tuple-element.390, bf16[2,2048,2048]{2,1,0:T(8,128)(2,1)S(1)} %bitcast.125, bf16[1,512,2048]{2,1,0:T(8,128)(2,1)S(1)} %copy-done), kind=kOutput, calls=%fused_computation.24 | convolution fusion | flops 4305453056 | bytes 14680064 | tf_op jit(solution)/shard_map/dot_general | solution.py:65
  28.8 1.3 fusion.34
  30.1 0.1 copy-done.4
  30.2 1.6 copy-done.11
  31.8 8.7 %multiply_convert_fusion.2 = bf16[512,2048]{1,0:T(8,128)(2,1)S(1)} fusion(f32[512,2048]{1,0:T(8,128)S(1)} %copy-done.11, bf16[512,2048]{1,0:T(8,128)(2,1)S(1)} %multiply_convert_fusion.3, bf16[2,2048,2048]{2,1,0:T(8,128)(2,1)} %param.37), kind=kOutput, calls=%fused_computation.23 | convolution fusion | flops 4304404480 | bytes 16777216 | tf_op jit(solution)/shard_map/dot_general | solution.py:76
  40.5 1.4 copy-done.7
  41.8 2.3 %fusion.39 = f32[512,512]{1,0:T(8,128)} fusion(f32[512,512]{1,0:T(8,128)S(1)} %fusion.34, f32[512,512]{1,0:T(8,128)S(1)} %convolution_multiply_fusion.6, bf16[512,2048]{1,0:T(8,128)(2,1)S(1)} %multiply_convert_fusion.2), kind=kOutput, calls=%fused_computation.42 | convolution fusion | flops 1074528256 | bytes 5242880 | tf_op jit(solution)/shard_map/dot_general | solution.py:88
  44.8 92.5 %conditional.4 = ((bf16[512,2048]{1,0:T(8,128)(2,1)}, bf16[512,2048]{1,0:T(8,128)(2,1)})) conditional(s32[]{:T(128)} %clamp.3, (bf16[512,2048]{1,0:T(8,128)(2,1)}, bf16[512,2048]{1,0:T(8,128)(2,1)S(1)}) %tuple.404, (bf16[512,2048]{1,0:T(8,128)(2,1)}, bf16[512,2048]{1,0:T(8,128)(2,1)S(1)}) %tuple.420, ...), branch_computations={%region_1.0_spmd, %region_2.0_spmd, %region_3.0_spmd, %region_4.0_... | conditional | bytes 8
  44.9 92.3 %swap_1.1 = (bf16[512,2048]{1,0:T(8,128)(2,1)}, bf16[512,2048]{1,0:T(8,128)(2,1)}) custom-call(bf16[512,2048]{1,0:T(8,128)(2,1)} %get-tuple-element.256.a_ref, bf16[512,2048]{1,0:T(8,128)(2,1)S(1)} %get-tuple-element.257.c_ref), custom_call_target="tpu_custom_call" | custom-call | tf_op jit(solution)/shard_map/cond/branch_0_fun/swap_1/pallas_call | solution.py:43
  137.4 7.9 %fusion.8 = f32[512,2048]{1,0:T(8,128)S(1)} fusion(bf16[512,2048]{1,0:T(8,128)(2,1)} %get-tuple-element.322, bf16[2,2048,2048]{2,1,0:T(8,128)(2,1)} %param.37), kind=kOutput, calls=%fused_computation.8 | convolution fusion | flops 4294967296 | bytes 14680064 | tf_op jit(solution)/shard_map/dot_general | solution.py:65
  145.4 1.4 convolution_multiply_fusion.1
  146.8 0.7 copy-done.10
  147.5 1.6 slice-done.7
  149.2 0.6 copy-done.3
  149.8 7.9 %fusion.18 = bf16[512,2048]{1,0:T(8,128)(2,1)S(1)} fusion(bf16[512,2048]{1,0:T(8,128)(2,1)S(1)} %copy-done.3, bf16[2,2048,2048]{2,1,0:T(8,128)(2,1)S(1)} %bitcast.127, f32[512,2048]{1,0:T(8,128)} %copy-done.10), kind=kOutput, calls=%fused_computation.19 | convolution fusion | flops 4310695936 | bytes 16777216 | tf_op jit(solution)/shard_map/dot_general | solution.py:65
  157.7 1.3 copy-done.6
  159.0 1.3 fusion.31
  160.3 12.8 %fusion.36 = f32[512,512]{1,0:T(8,128)} fusion(bf16[512,2048]{1,0:T(8,128)(2,1)} %copy-done.7, f32[512,2048]{1,0:T(8,128)} %copy-done.10, bf16[512,2048]{1,0:T(8,128)(2,1)} %copy-done.6, bf16[2,2048,2048]{2,1,0:T(8,128)(2,1)} %param.37), kind=kOutput, calls=%fused_computation.41 | convolution fusion | flops 5378408448 | bytes 17825792 | tf_op jit(solution)/shard_map/dot_general | solution.py:88
  173.1 4.1 %fusion.40 = f32[512,512]{1,0:T(8,128)} fusion(f32[512,512]{1,0:T(8,128)S(1)} %fusion.31, f32[512,512]{1,0:T(8,128)} %fusion.36, bf16[512,2048]{1,0:T(8,128)(2,1)} %get-tuple-element.322, bf16[1,512,2048]{2,1,0:T(8,128)(2,1)S(1)} %copy-done.2), kind=kOutput, calls=%fused_computation.43 | convolution fusion | flops 1074528256 | bytes 7340032 | tf_op jit(solution)/shard_map/dot_general | solution.py:87
  177.3 35.7 %reduce-scatter.5.cloned.1.call-done = f32[128,512]{1,0:T(8,128)} async-done(((f32[512,512]{1,0:T(8,128)}), f32[128,512]{1,0:T(8,128)}) %reduce-scatter.5.cloned.1.call-update) | async-done | bytes 262160 | tf_op jit(solution)/shard_map/reduce_scatter | solution.py:105
  (39 shorter events, 0.2 us)
Async XLA Ops:
  7.2 3.7 %copy-start.1 = (bf16[1,512,2048]{2,1,0:T(8,128)(2,1)S(1)}, bf16[1,512,2048]{2,1,0:T(8,128)(2,1)}, u32[]{:S(2)}) copy-start(bf16[1,512,2048]{2,1,0:T(8,128)(2,1)} %param.35) | copy-start | bytes 6291460
  7.2 170.1 %reduce-scatter.3.cloned.1.call-start = ((), (), s32[]{:S(2)}) async-start(), calls=%async_computation.2 | async-start | bytes 1310720 | tf_op jit(solution)/shard_map/reduce_scatter | solution.py:104
  7.2 14.8 %slice-start = ((s8[16777216]{0:T(1024)(128)(4,1)}), s8[4194304]{0:T(1024)(128)(4,1)S(1)}, s32[]{:S(2)}) async-start(s8[16777216]{0:T(1024)(128)(4,1)} %bitcast.124), calls=%async_computation.4 | async-start | bytes 8388608
  10.9 11.1 %slice-start.1 = ((s8[16777216]{0:T(1024)(128)(4,1)}), s8[4194304]{0:T(1024)(128)(4,1)S(1)}, s32[]{:S(2)}) async-start(s8[16777216]{0:T(1024)(128)(4,1)} %bitcast.124), calls=%async_computation.5 | async-start | bytes 8388608
  10.9 11.1 %slice-start.2 = ((s8[16777216]{0:T(1024)(128)(4,1)}), s8[4194304]{0:T(1024)(128)(4,1)S(1)}, s32[]{:S(2)}) async-start(s8[16777216]{0:T(1024)(128)(4,1)} %bitcast.124), calls=%async_computation.6 | async-start | bytes 8388608
  10.9 11.1 %slice-start.3 = ((s8[16777216]{0:T(1024)(128)(4,1)}), s8[4194304]{0:T(1024)(128)(4,1)S(1)}, s32[]{:S(2)}) async-start(s8[16777216]{0:T(1024)(128)(4,1)} %bitcast.124), calls=%async_computation.7 | async-start | bytes 8388608
  20.7 1.3 copy-start.8
  20.7 2.3 %copy-start = (bf16[1,512,2048]{2,1,0:T(8,128)(2,1)S(1)}, bf16[1,512,2048]{2,1,0:T(8,128)(2,1)}, u32[]{:S(2)}) copy-start(bf16[1,512,2048]{2,1,0:T(8,128)(2,1)} %param.36) | copy-start | bytes 6291460
  28.8 1.4 copy-start.4
  28.8 2.9 %copy-start.11 = (f32[512,2048]{1,0:T(8,128)S(1)}, f32[512,2048]{1,0:T(8,128)}, u32[]{:S(2)}) copy-start(f32[512,2048]{1,0:T(8,128)} %get-tuple-element.391) | copy-start | bytes 12582916
  40.4 1.4 copy-start.7
  44.1 168.8 %reduce-scatter.5.cloned.1.call-start = ((), (), s32[]{:S(2)}) async-start(), calls=%async_computation.3 | async-start | bytes 1310720 | tf_op jit(solution)/shard_map/reduce_scatter | solution.py:105
  137.4 8.0 %copy-start.9 = (bf16[512,2048]{1,0:T(8,128)(2,1)S(1)}, bf16[512,2048]{1,0:T(8,128)(2,1)}, u32[]{:S(2)}) copy-start(bf16[512,2048]{1,0:T(8,128)(2,1)} %copy-done.8) | copy-start | bytes 6291460
  137.4 10.1 %slice-start.4 = ((s8[16777216]{0:T(1024)(128)(4,1)}), s8[4194304]{0:T(1024)(128)(4,1)S(1)}, s32[]{:S(2)}) async-start(s8[16777216]{0:T(1024)(128)(4,1)} %bitcast.126), calls=%async_computation.8 | async-start | bytes 8388608
  137.4 10.1 %slice-start.5 = ((s8[16777216]{0:T(1024)(128)(4,1)}), s8[4194304]{0:T(1024)(128)(4,1)S(1)}, s32[]{:S(2)}) async-start(s8[16777216]{0:T(1024)(128)(4,1)} %bitcast.126), calls=%async_computation.9 | async-start | bytes 8388608
  137.4 10.1 %slice-start.6 = ((s8[16777216]{0:T(1024)(128)(4,1)}), s8[4194304]{0:T(1024)(128)(4,1)S(1)}, s32[]{:S(2)}) async-start(s8[16777216]{0:T(1024)(128)(4,1)} %bitcast.126), calls=%async_computation.10 | async-start | bytes 8388608
  145.4 2.1 copy-start.10
  145.4 3.8 %slice-start.7 = ((s8[16777216]{0:T(1024)(128)(4,1)}), s8[4194304]{0:T(1024)(128)(4,1)S(1)}, s32[]{:S(2)}) async-start(s8[16777216]{0:T(1024)(128)(4,1)} %bitcast.126), calls=%async_computation.11 | async-start | bytes 8388608
  145.4 4.4 %copy-start.3 = (bf16[512,2048]{1,0:T(8,128)(2,1)S(1)}, bf16[512,2048]{1,0:T(8,128)(2,1)}, u32[]{:S(2)}) copy-start(bf16[512,2048]{1,0:T(8,128)(2,1)} %get-tuple-element.389) | copy-start | bytes 6291460
  149.8 9.2 %copy-start.5 = (bf16[512,2048]{1,0:T(8,128)(2,1)S(1)}, bf16[512,2048]{1,0:T(8,128)(2,1)}, u32[]{:S(2)}) copy-start(bf16[512,2048]{1,0:T(8,128)(2,1)} %copy-done.4) | copy-start | bytes 6291460
  157.6 1.3 copy-start.6
  160.2 12.8 %copy-start.2 = (bf16[1,512,2048]{2,1,0:T(8,128)(2,1)S(1)}, bf16[1,512,2048]{2,1,0:T(8,128)(2,1)}, u32[]{:S(2)}) copy-start(bf16[1,512,2048]{2,1,0:T(8,128)(2,1)} %param.35) | copy-start | bytes 6291460
Sparse Core Ops, SparseCore 0:
  44.3 35.1 reduce-scatter.2
  177.3 35.5 reduce-scatter.4
